TPU v7x, 128 devices: a whole 4x4x4 slice. The times are simulated.
128 devices in a mesh: group: 8 (over x, y_hi), fsdp: 16 (over y_lo, z, core).
Axes of the slice: x: 4, y: 4 (y_hi: 2, y_lo: 2; y = y_hi * 2 + y_lo), z: 4, core: 2. Of those that a mesh axis runs over, the one named last changes fastest.
Arguments:
- tokens: bfloat16 [65536, 8192], P(('group', 'fsdp')), may hold values from -60 to 60
- norm_gain: bfloat16 [8, 8192], P('group', 'fsdp'), may hold values from 0.099609375 to 1.8984375
- value_weight: bfloat16 [8, 8192, 512], P('group', 'fsdp'), may hold values from -0.125 to 0.125
- cotangent: bfloat16 [65536, 512], P(('group', 'fsdp')), may hold values from -0.59765625 to 0.59765625
- pseudo_grad: bfloat16 [8, 2048, 8192], P('group', 'fsdp'), may hold values from -6 to 6
- outer_params: float32 [2048, 8192], P('fsdp', 'group'), may hold values from -6 to 6
- momentum: float32 [2048, 8192], P('fsdp', 'group'), may hold values from -3 to 3
Outputs:
- values: bfloat16 [65536, 512], P(('group', 'fsdp'))
- token_grad: bfloat16 [65536, 8192], P(('group', 'fsdp'))
- weight_grad: float32 [8, 8192, 512], P('group', 'fsdp')
- gain_grad: float32 [8, 8192], P('group', 'fsdp')
- new_global: float32 [2048, 8192], P('fsdp', 'group')
- new_momentum: float32 [2048, 8192], P('fsdp', 'group')
- new_params: bfloat16 [2048, 8192], P('fsdp')
All inputs are finite; a program needn't handle non-finite values.
Results may differ from a plain program's by a relative error of at most 0.012.
Values may be sent and summed in bfloat16 or wider, within the bound.
A program may use at most 192 MiB of HBM per device.

v0:
```python
import jax
import jax.numpy as jnp
from jax import lax
from jax.sharding import PartitionSpec as P

epsilon = 1e-05
outer_rate = 0.7
momentum_decay = 0.9


def shards(tokens, norm_gain, value_weight, cotangent, pseudo_grad, outer_params, momentum):
    outer_terms = pseudo_grad[0].astype(jnp.float32)
    whole_sum = lax.psum(outer_terms.astype(jnp.bfloat16), "group").astype(jnp.float32)
    share_width = outer_params.shape[1]
    summed = lax.dynamic_slice_in_dim(
        whole_sum, lax.axis_index("group") * share_width, share_width, 1
    )
    average = summed / lax.axis_size("group")
    new_momentum = momentum_decay * momentum + average
    new_global = outer_params - outer_rate * (average + momentum_decay * new_momentum)
    new_params = lax.all_gather(new_global.astype(jnp.bfloat16), "group", axis=1, tiled=True)
    wide_tokens = tokens.astype(jnp.float32)
    inv_rms = lax.rsqrt(jnp.mean(wide_tokens * wide_tokens, axis=1, keepdims=True) + epsilon)
    scaled = wide_tokens * inv_rms
    weight_piece = lax.all_gather(value_weight, "fsdp", axis=1, tiled=True)
    gain_piece = lax.all_gather(norm_gain, "fsdp", axis=1, tiled=True)
    hidden_piece = (scaled * gain_piece[0].astype(jnp.float32)[None, :]).astype(jnp.bfloat16)
    acc_values = jnp.dot(hidden_piece, weight_piece[0], preferred_element_type=jnp.float32)
    gain_all = gain_piece[0]
    projected, hidden, gain_all = (acc_values, hidden_piece, gain_all)
    gain_row = gain_all.astype(jnp.float32)[None, :]
    hidden_grad = lax.dot_general(
        cotangent,
        lax.all_gather(value_weight, "fsdp", axis=1, tiled=True)[0],
        (((1,), (1,)), ((), ())),
        preferred_element_type=jnp.float32,
    )
    weight_term = lax.dot_general(
        hidden, cotangent, (((0,), (0,)), ((), ())), preferred_element_type=jnp.float32
    )
    gain_term = jnp.sum(scaled * hidden_grad, axis=0)
    weight_share, gain_share = (
        lax.psum_scatter(weight_term, "fsdp", scatter_dimension=0, tiled=True),
        lax.psum_scatter(gain_term, "fsdp", scatter_dimension=0, tiled=True),
    )
    gained = gain_row * hidden_grad
    token_grad = inv_rms * (gained - scaled * jnp.mean(scaled * gained, axis=1, keepdims=True))
    return (
        projected.astype(jnp.bfloat16),
        token_grad.astype(jnp.bfloat16),
        weight_share[None],
        gain_share[None],
        new_global,
        new_momentum,
        new_params,
    )


def solution(mesh):
    placed = (
        P(("group", "fsdp"), None),
        P("group", "fsdp"),
        P("group", "fsdp", None),
        P(("group", "fsdp"), None),
        P("group", "fsdp", None),
        P("fsdp", "group"),
        P("fsdp", "group"),
    )
    return jax.shard_map(
        shards,
        mesh=mesh,
        in_specs=placed,
        out_specs=(
            P(("group", "fsdp"), None),
            P(("group", "fsdp"), None),
            P("group", "fsdp", None),
            P("group", "fsdp"),
            P("fsdp", "group"),
            P("fsdp", "group"),
            P("fsdp", None),
        ),
        check_vma=False,
    )
```

profile of v0, /device:TPU:0, one launch (start us, length us, event | category | flops | bytes accessed | tf_op | source)
XLA Modules:
  0.0 344.6 jit_solution(17397478203507357667)
XLA Ops:
  7.2 0.0 copy-start
  7.2 0.0 all-reduce.3.cloned.1.call-start
  7.2 0.7 all-reduce.3.cloned.1.call-update
  7.9 0.0 all-gather.5.cloned.1.call-start
  8.0 115.0 %all-reduce.3.cloned.1.call-done = bf16[128,8192]{1,0:T(8,128)(2,1)} async-done(((bf16[128,8192]{1,0:T(8,128)(2,1)}), bf16[128,8192]{1,0:T(8,128)(2,1)}) %all-reduce.3.cloned.1.call-update) | async-done | bytes 2097168 | tf_op jit(solution)/shard_map/psum | solution.py:13
  122.9 2.5 fusion.23
  125.5 0.0 all-gather.5.cloned.1.call-update
  125.5 0.0 all-gather.3.cloned.1.call-start
  125.5 0.7 all-gather.3.cloned.1.call-update
  126.2 0.0 reduce-scatter.2.cloned.1.call-start
  126.3 19.5 %all_gather.10 = bf16[1,8192]{1,0:T(2,128)(2,1)S(1)} all-gather(bf16[1,512]{1,0:T(2,128)(2,1)} %param.8), channel_id=1, replica_groups=mesh['group'=8,'fsdp'=16] {'fsdp'}, dimensions={1}, use_global_device_ids=true | all-gather | bytes 17408 | tf_op jit(solution)/shard_map/all_gather | solution.py:26
  145.8 5.1 %fusion.10 = f32[512]{0:T(512)S(1)} fusion(bf16[512,8192]{1,0:T(8,128)(2,1)} %param.7), kind=kLoop, calls=%fused_computation.12 | loop fusion | flops 12582400 | bytes 8390656 | tf_op jit(solution)/shard_map/reduce_sum | solution.py:23
  151.0 0.0 copy-done
  151.0 13.4 %fusion.15 = f32[8192,512]{1,0:T(8,128)} fusion(bf16[512,512]{1,0:T(8,128)(2,1)S(1)} %copy-done, bf16[512,8192]{1,0:T(8,128)(2,1)} %param.7, f32[8192]{0:T(1024)S(1)} %bitcast.17, f32[512]{0:T(512)S(1)} %add_rsqrt_fusion), kind=kOutput, calls=%fused_computation.17 | convolution fusion | flops 4311744512 | bytes 25724928 | tf_op jit(solution)/shard_map/dot_general | solution.py:38
  164.3 0.0 copy-start.4
  164.3 0.0 reduce-scatter.2.cloned.1.call-update
  164.4 0.6 copy-done.4
  165.0 0.6 dynamic-slice
  166.2 14.6 %all-gather.5.cloned.1.call-done = bf16[128,8192]{1,0:T(8,128)(2,1)} async-done(((bf16[128,1024]{1,0:T(8,128)(2,1)}), bf16[128,8192]{1,0:T(8,128)(2,1)}) %all-gather.5.cloned.1.call-update) | async-done | bytes 2097168 | tf_op jit(solution)/shard_map/all_gather | solution.py:21
  180.9 52.8 %all-gather.3.cloned.1.call-done = bf16[1,8192,512]{2,1,0:T(8,128)(2,1)} async-done(((bf16[1,512,512]{2,1,0:T(8,128)(2,1)}), bf16[1,8192,512]{2,1,0:T(8,128)(2,1)}) %all-gather.3.cloned.1.call-update) | async-done | bytes 8388624 | tf_op jit(solution)/shard_map/all_gather | solution.py:25
  233.7 13.3 %fusion.9 = (f32[8192]{0:T(1024)S(1)}, f32[512]{0:T(512)S(1)}, f32[512,8192]{1,0:T(8,128)}) fusion(bf16[512,8192]{1,0:T(8,128)(2,1)} %param.7, f32[512]{0:T(512)S(1)} %add_rsqrt_fusion, f32[8192]{0:T(1024)S(1)} %bitcast.18, bf16[512,512]{1,0:T(8,128)(2,1)S(1)} %copy-done, bf16[1,8192,512]{2,1,0:T(8,128)(2,1)} %all-gather.3.cloned.1.call-done), kind=kOutput, calls=%fused_computation.11 | convolution fusion | flops 4324318720 | bytes 34148352 | tf_op jit(solution)/shard_map/dot_general | solution.py:32
  246.9 57.2 %all-reduce = f32[8192]{0:T(1024)S(1)} all-reduce(f32[8192]{0:T(1024)S(1)} %get-tuple-element.7), channel_id=3, replica_groups=mesh['group'=8,'fsdp'=16] {'fsdp'}, use_global_device_ids=true, to_apply=%region_4.0.clone | all-reduce | flops 8192 | bytes 65536
  304.2 0.7 dynamic-slice.1
  304.8 0.0 copy-start.2
  304.8 11.6 %fusion.18 = bf16[512,512]{1,0:T(8,128)(2,1)} fusion(bf16[1,8192,512]{2,1,0:T(8,128)(2,1)} %all-gather.3.cloned.1.call-done, bf16[512,8192]{1,0:T(8,128)(2,1)} %param.7, f32[8192]{0:T(1024)S(1)} %bitcast.19, f32[512]{0:T(512)S(1)} %add_rsqrt_fusion), kind=kOutput, calls=%fused_computation.18 | convolution fusion | flops 4312006656 | bytes 17336320 | tf_op jit(solution)/shard_map/dot_general | solution.py:28
  316.4 0.0 copy-start.1
  316.4 0.0 copy-done.2
  316.4 9.5 %fusion.8 = bf16[512,8192]{1,0:T(8,128)(2,1)} fusion(bf16[512,8192]{1,0:T(8,128)(2,1)} %param.7, f32[512,8192]{1,0:T(8,128)S(1)} %copy-done.2, f32[512]{0:T(512)S(1)} %broadcast_multiply_fusion, f32[8192]{0:T(1024)S(1)} %bitcast.20, f32[512]{0:T(512)S(1)} %add_rsqrt_fusion), kind=kLoop, calls=%fused_computation.10 | loop fusion | flops 29360128 | bytes 33591296 | tf_op jit(solution)/shard_map/convert_element_type | solution.py:50
  325.9 10.8 %reduce-scatter.2.cloned.1.call-done = f32[512,512]{1,0:T(8,128)} async-done(((f32[8192,512]{1,0:T(8,128)}), f32[512,512]{1,0:T(8,128)}) %reduce-scatter.2.cloned.1.call-update) | async-done | bytes 1048592 | tf_op jit(solution)/shard_map/reduce_scatter | solution.py:43
  336.7 0.0 copy-done.3
  336.7 1.3 copy.17
  338.0 0.0 copy-done.1
  (4 shorter events, 0.0 us)
Async XLA Ops:
  7.2 143.8 %copy-start = (bf16[512,512]{1,0:T(8,128)(2,1)S(1)}, bf16[512,512]{1,0:T(8,128)(2,1)}, u32[]{:S(2)}) copy-start(bf16[512,512]{1,0:T(8,128)(2,1)} %param.10) | copy-start | bytes 1572868
  7.2 115.7 %all-reduce.3.cloned.1.call-start = ((), (), s32[]{:S(2)}) async-start(), calls=%async_computation.3 | async-start | bytes 4194304 | tf_op jit(solution)/shard_map/psum | solution.py:13
  7.9 173.0 %all-gather.5.cloned.1.call-start = ((), (), s32[]{:S(2)}) async-start(), calls=%async_computation.4 | async-start | bytes 2359296 | tf_op jit(solution)/shard_map/all_gather | solution.py:21
  125.5 108.2 %all-gather.3.cloned.1.call-start = ((), (), s32[]{:S(2)}) async-start(), calls=%async_computation.1 | async-start | bytes 8912896 | tf_op jit(solution)/shard_map/all_gather | solution.py:25
  126.2 210.5 %reduce-scatter.2.cloned.1.call-start = ((), (), s32[]{:S(2)}) async-start(), calls=%async_computation.2 | async-start | bytes 17825792 | tf_op jit(solution)/shard_map/reduce_scatter | solution.py:43
  164.3 0.7 copy-start.4
  304.8 11.6 %copy-start.2 = (f32[512,8192]{1,0:T(8,128)S(1)}, f32[512,8192]{1,0:T(8,128)}, u32[]{:S(2)}) copy-start(f32[512,8192]{1,0:T(8,128)} %get-tuple-element.12) | copy-start | bytes 50331652
  316.4 21.6 %copy-start.1 = (bf16[512,512]{1,0:T(8,128)(2,1)S(1)}, bf16[512,512]{1,0:T(8,128)(2,1)}, u32[]{:S(2)}) copy-start(bf16[512,512]{1,0:T(8,128)(2,1)} %param.10) | copy-start | bytes 1572868
  316.4 20.3 %copy-start.3 = (bf16[128,8192]{1,0:T(8,128)(2,1)S(1)}, bf16[128,8192]{1,0:T(8,128)(2,1)}, u32[]{:S(2)}) copy-start(bf16[128,8192]{1,0:T(8,128)(2,1)} %all-gather.5.cloned.1.call-done) | copy-start | bytes 6291460
Sparse Core Ops, SparseCore 0:
  10.5 112.3 all-reduce.2
  125.9 54.9 all-gather.4
  182.6 51.0 all-gather.2
  236.5 100.1 reduce-scatter.1
where the time goes:
time: 345 us
  waiting for transfers between devices  195 us (57%)
  blocking collectives  76.7 us (22%)
  matrix products  38.3 us (11%)
  other arithmetic  17.2 us (5%)
  between operations  14.4 us (4%)
    psum x1, waiting for transfers between devices, shards(): lax.psum(outer_terms.astype(jnp.bfloat16), 'group').astype(jnp.float32)  115 us
    unnamed x1, blocking collectives  57.2 us
    all_gather x1, waiting for transfers between devices, shards(): weight_piece = lax.all_gather(value_weight, 'fsdp', axis=1, tiled=True)  52.8 us
    all_gather x1, blocking collectives, shards(): gain_piece = lax.all_gather(norm_gain, 'fsdp', axis=1, tiled=True)  19.5 us
    all_gather x1, waiting for transfers between devices, shards(): lax.all_gather(new_global.astype(jnp.bfloat16), 'group', axis=1, tiled=True)  14.6 us
    dot_general x1, matrix products, shards(): lax.dot_general(hidden, cotangent, (((0,), (0,)), ((), ())), preferred_el...  13.4 us
    dot_general x1, matrix products, shards(): lax.dot_general(cotangent, lax.all_gather(value_weight, 'fsdp', axis=1, t...  13.3 us
    dot_general x1, matrix products, shards(): jnp.dot(hidden_piece, weight_piece[0], preferred_element_type=jnp.float32)  11.6 us
  transfers between devices with their start and end apart: 4, of which 4 were waited for; matrix products, arithmetic and copies ran while one was open for 16% of the time, Pallas kernels for 0%

commit v1 on v0

v1 whole, which is shorter than its diff:
```python
import functools

import jax
import jax.numpy as jnp
from jax import lax
from jax.experimental import pallas as pl
from jax.experimental.pallas import tpu as pltpu
from jax.sharding import PartitionSpec as P

epsilon = 1e-05
outer_rate = 0.7
momentum_decay = 0.9

F32 = jnp.float32
BF16 = jnp.bfloat16

D = 8192
T = 512
B = 512
K = 512
H = B // 2
N_FSDP = 16
ROWS = 128
SHARE = 1024
PARTS = 2
PR = ROWS // PARTS
K1 = 320
K2 = K - K1
CHUNK = 1024
N_CHUNK = D // CHUNK
N_COPIES = 96


def kernel(
    tok_hbm, gain_ref, w_hbm, cot_hbm, pg_hbm, op_hbm, mo_hbm,
    val_o, tg_o, wgr_o, gg_o, ng_o, nm_o, np_o,
    tok, sibtok, wall, gs, ry, ryz, rh0, rh1, rz0, rz1,
    w_v, wt, cot_v, cps, cott, acc, sq, inv_v, wgv,
    px, pown, pys, pyr, psum, op_v, mo_v, ng_v, nm_v, np_v, val_v,
    ssem, rsem, lsem,
):
    group = lax.axis_index("group")
    fs = lax.axis_index("fsdp")
    x, yh = group // 2, group % 2
    yl, z, c = fs // 8, (fs // 2) % 4, fs % 2

    def at(dx=0, dyh=0, dyl=0, dz=0, dc=0):
        return (
            ((x + dx) % 4) * 2 + (yh + dyh) % 2,
            ((yl + dyl) % 2) * 8 + ((z + dz) % 4) * 2 + (c + dc) % 2,
        )

    SIB, YP, ZP, ZM, Y2 = at(dc=1), at(dyl=1), at(dz=1), at(dz=3), at(dyh=1)
    XS = {1: at(dx=1), 3: at(dx=3), 2: at(dx=2)}

    def col(dy, dz, dc):
        owner = ((yl + dy) % 2) * 8 + ((z + dz) % 4) * 2 + (c + dc) % 2
        return pl.multiple_of(owner * B, B)

    def slot(dy, dz, dc):
        return dy * 8 + dz * 2 + dc

    started = []
    locals_ = []

    def send(src, dst, to):
        n = len(started)
        copy = pltpu.make_async_remote_copy(
            src_ref=src, dst_ref=dst, send_sem=ssem.at[n], recv_sem=rsem.at[n],
            device_id=to, device_id_type=pl.DeviceIdType.MESH,
        )
        copy.start()
        started.append(copy)
        return copy

    def local(src, dst):
        copy = pltpu.make_async_copy(src, dst, lsem.at[len(locals_)])
        copy.start()
        locals_.append(copy)
        return copy

    load_w = local(w_hbm.at[0], w_v)
    load_tok = [
        local(tok_hbm.at[:, pl.ds(i * CHUNK, CHUNK)], tok.at[:, pl.ds(i * CHUNK, CHUNK)])
        for i in range(N_CHUNK)
    ]
    load_cot = local(cot_hbm, cot_v)
    wide_cols = pl.ds(pl.multiple_of(x * 2 * SHARE, 2 * SHARE), 2 * SHARE)
    load_pg = local(pg_hbm.at[0, :, wide_cols], pown)
    load_op = local(op_hbm, op_v)
    load_mo = local(mo_hbm, mo_v)

    barrier = pltpu.get_barrier_semaphore()
    partners = [SIB, YP, ZP, ZM, Y2, XS[1], XS[3], XS[2]]
    for to in partners:
        pl.semaphore_signal(barrier, inc=1, device_id=to, device_id_type=pl.DeviceIdType.MESH)

    load_w.wait()
    gain_row = gain_ref[...].astype(F32)
    gain_col = jnp.transpose(jnp.broadcast_to(gain_row, (128, B)))
    wall[0] = (w_v[...].astype(F32) * jnp.concatenate([gain_col] * 4, axis=1)).astype(BF16)

    pl.semaphore_wait(barrier, len(partners))

    def half(s, h):
        return wall.at[s, pl.ds(h * H, H)]

    def along_z(dy):
        own = slot(dy, 0, 0)
        zp, zm = slot(dy, 3, 0), slot(dy, 1, 0)
        got = {}
        for k in range(2):
            got["p", 1 - k] = send(half(own, 1 - k), half(zp, 1 - k), ZP)
            got["m", k] = send(half(own, k), half(zm, k), ZM)
        return got

    def to_sibling(dy, dz):
        return send(wall.at[slot(dy, dz, 0)], wall.at[slot(dy, dz, 1)], SIB)

    sib = {}
    yp = [send(half(0, h), half(slot(1, 0, 0), h), YP) for h in range(2)]
    az = {0: along_z(0)}
    ORDER = [(dy, dz) for dz in (2, 1, 3, 0) for dy in (1, 0)]
    st = {}
    for dy, dz in ORDER[:4]:
        st[dy, dz] = send(
            tok_hbm.at[:, pl.ds(col(dy, dz, 1), B)], sibtok.at[dy * 4 + dz], SIB
        )
    sib[0, 0] = to_sibling(0, 0)
    for dy, dz in ORDER[4:]:
        st[dy, dz] = send(
            tok_hbm.at[:, pl.ds(col(dy, dz, 1), B)], sibtok.at[dy * 4 + dz], SIB
        )

    def rows(p):
        return pl.ds(p * PR, PR)

    xs = {}
    for p in range(PARTS):
        for dx in (1, 3, 2):
            theirs = pl.ds(pl.multiple_of(((x + dx) % 4) * 2 * SHARE, 2 * SHARE), 2 * SHARE)
            xs[p, dx] = send(pg_hbm.at[0, rows(p), theirs], px.at[p, dx - 1], XS[dx])

    sq[...] = jnp.zeros_like(sq)
    for i in range(N_CHUNK):
        load_tok[i].wait()

        def squares(r, _, i=i):
            rr = pl.ds(r * 64, 64)
            wide = tok[rr, pl.ds(i * CHUNK, CHUNK)].astype(F32)
            wide = wide * wide
            total = wide[:, :128]
            for l in range(1, CHUNK // 128):
                total = total + wide[:, l * 128:(l + 1) * 128]
            sq[rr, :] += total
            return 0

        lax.fori_loop(0, T // 64, squares, 0)
    load_cot.wait()
    inv = lax.rsqrt(jnp.sum(sq[...], axis=1, keepdims=True) * (1.0 / D) + epsilon)
    inv_v[...] = inv
    scaled_cot = cot_v[...].astype(F32) * inv
    cps[...] = scaled_cot.astype(BF16)
    cott[0] = jnp.transpose(scaled_cot).astype(BF16)
    ct = send(cott.at[0], cott.at[1], SIB)

    def products(dy, dz):
        st[dy, dz].wait_recv()
        own = jnp.dot(cott[0], tok[:, pl.ds(col(dy, dz, 0), B)], preferred_element_type=F32)
        other = jnp.dot(cott[1], sibtok[dy * 4 + dz], preferred_element_type=F32)
        gs[dy, dz] = (own + other).astype(BF16)

    SEG = {0: (0, 0, K1), 1: (0, K1, K2), 2: (1, K1, K2)}
    seg_rh0 = {0: rh0.at[0, :K1 // 2], 1: rh0.at[1, :K2 // 2], 2: rh0.at[2, :K2 // 2]}
    seg_rh1 = {0: rh1.at[0, :K1 // 2], 1: rh1.at[1, :K2 // 2], 2: rh1.at[2, :K2 // 2]}
    seg_rz0 = {0: rz0.at[0, :K1], 1: rz0.at[1, :K2], 2: rz0.at[2, :K2]}
    seg_rz1 = {0: rz1.at[0, :K1], 1: rz1.at[1, :K2], 2: rz1.at[2, :K2]}

    def far_halves(g):
        dy, r0, n = SEG[g]
        m = n // 2
        return (
            send(gs.at[dy, 2, pl.ds(r0, m)], seg_rh0[g], ZP),
            send(gs.at[dy, 2, pl.ds(r0 + m, m)], seg_rh1[g], ZM),
        )

    def add_into(ref, other):
        ref[...] = (ref[...].astype(F32) + other[...].astype(F32)).astype(BF16)

    def near_free(g):
        dy, r0, n = SEG[g]
        m = n // 2
        return [
            send(gs.at[dy, 1, pl.ds(r0 + m, m)], seg_rz0[g].at[pl.ds(m, m)], ZP),
            send(gs.at[dy, 3, pl.ds(r0, m)], seg_rz1[g].at[pl.ds(0, m)], ZM),
        ]

    def near_joined(g, far):
        dy, r0, n = SEG[g]
        m = n // 2
        far[0].wait_recv()
        add_into(gs.at[dy, 1, pl.ds(r0, m)], seg_rh0[g])
        a = send(gs.at[dy, 1, pl.ds(r0, m)], seg_rz0[g].at[pl.ds(0, m)], ZP)
        far[1].wait_recv()
        add_into(gs.at[dy, 3, pl.ds(r0 + m, m)], seg_rh1[g])
        b = send(gs.at[dy, 3, pl.ds(r0 + m, m)], seg_rz1[g].at[pl.ds(m, m)], ZM)
        return [a, b]

    def across_y(dz):
        return send(gs.at[1, dz, pl.ds(0, K1)], ry.at[dz], YP)

    def join_y(dz):
        rys[dz].wait_recv()
        add_into(gs.at[0, dz, pl.ds(0, K1)], ry.at[dz])

    rys, far = {}, {}
    ct.wait_recv()
    products(1, 2)
    rys[2] = across_y(2)
    products(0, 2)
    far[1], far[2] = far_halves(1), far_halves(2)
    for dy, dz in ORDER[2:]:
        products(dy, dz)

    acc[...] = jnp.zeros_like(acc)

    def forward(dy, dz, dc):
        acc[...] += jnp.dot(
            tok[:, pl.ds(col(dy, dz, dc), B)], wall[slot(dy, dz, dc)], preferred_element_type=F32
        )

    def far_forward(dy):
        az[dy]["m", 0].wait_recv()
        a = send(half(slot(dy, 1, 0), 0), half(slot(dy, 2, 0), 0), ZM)
        az[dy]["p", 1].wait_recv()
        b = send(half(slot(dy, 3, 0), 1), half(slot(dy, 2, 0), 1), ZP)
        return a, b

    def rest_of_near(dy):
        az[dy]["m", 1].wait_recv()
        sib[dy, 1] = to_sibling(dy, 1)
        az[dy]["p", 0].wait_recv()
        sib[dy, 3] = to_sibling(dy, 3)

    def rest_of_far(dy):
        for copy in afar[dy]:
            copy.wait_recv()
        sib[dy, 2] = to_sibling(dy, 2)

    afar = {}
    yp[0].wait_recv()
    yp[1].wait_recv()
    az[1] = along_z(1)
    afar[0] = far_forward(0)
    sib[1, 0] = to_sibling(1, 0)
    rest_of_near(0)
    forward(0, 0, 0)
    sib[0, 0].wait_recv()
    forward(0, 0, 1)

    other_cols = pl.ds(pl.multiple_of((1 - yh) * SHARE, SHARE), SHARE)
    own_cols = pl.ds(pl.multiple_of(yh * SHARE, SHARE), SHARE)

    def outer_sum(p):
        for dx in (1, 3, 2):
            xs[p, dx].wait_recv()

        def total(cols):
            t = pown[rows(p), cols].astype(F32)
            for k in range(3):
                t = t + px[p, k, :, cols].astype(F32)
            return t

        pys[p] = total(other_cols).astype(BF16)
        copy = send(pys.at[p], pyr.at[p], Y2)
        psum[p] = total(own_cols)
        return copy

    def share_cols(dyh):
        return pl.ds(pl.multiple_of((x * 2 + (yh + dyh) % 2) * SHARE, SHARE), SHARE)

    def outer_step(p):
        y2s[p].wait_recv()
        rr = rows(p)
        average = (psum[p] + pyr[p].astype(F32)) * 0.125
        new_momentum = momentum_decay * mo_v[rr] + average
        new_global = op_v[rr] - outer_rate * (average + momentum_decay * new_momentum)
        nm_v[rr] = new_momentum
        ng_v[rr] = new_global
        np_v[rr] = new_global.astype(BF16)
        place = np_o.at[rr, share_cols(0)]
        npy[p] = send(np_v.at[rr], place, Y2)
        for dx in (1, 3, 2):
            npx[p, dx] = send(np_v.at[rr], place, XS[dx])
        local(np_v.at[rr], place)
        local(nm_v.at[rr], nm_o.at[rr])
        local(ng_v.at[rr], ng_o.at[rr])

    def spread_params(p):
        npy[p].wait_recv()
        place = np_o.at[rows(p), share_cols(1)]
        for dx in (1, 3, 2):
            npf[p, dx] = send(place, place, XS[dx])

    y2s, npy, npx, npf = {}, {}, {}, {}
    load_pg.wait()
    load_op.wait()
    load_mo.wait()
    y2s[0] = outer_sum(0)
    rys[1] = across_y(1)
    forward(1, 0, 0)
    forward(0, 1, 0)
    forward(0, 3, 0)
    for s in ((1, 0), (0, 1), (0, 3)):
        sib[s].wait_recv()
        forward(*s, 1)
    wt[...] = jnp.transpose(w_v[...].astype(F32))
    y2s[1] = outer_sum(1)
    outer_step(0)
    rys[3] = across_y(3)

    join_y(2)
    afar[1] = far_forward(1)
    rest_of_near(1)
    far[0] = far_halves(0)
    near = {g: near_free(g) + near_joined(g, far[g]) for g in (2, 1)}
    forward(1, 1, 0)
    forward(1, 3, 0)
    join_y(1)
    rest_of_far(0)
    outer_step(1)
    rys[0] = across_y(0)
    forward(0, 2, 0)
    for s in ((1, 1), (1, 3), (0, 2)):
        sib[s].wait_recv()
        forward(*s, 1)
    spread_params(0)
    rest_of_far(1)
    forward(1, 2, 0)
    sib[1, 2].wait_recv()
    forward(1, 2, 1)

    inv = inv_v[...]
    acc_v = acc[...]
    val_v[...] = (acc_v * inv).astype(BF16)
    local(val_v, val_o)
    inner = jnp.sum(cot_v[...].astype(F32) * acc_v, axis=1, keepdims=True)
    inv_v[...] = inv * inv * inv * inner * (1.0 / D)

    def backward(s, _):
        owner = ((yl + s // 8) % 2) * 8 + ((z + (s // 2) % 4) % 4) * 2 + (c + s % 2) % 2
        cols = pl.ds(pl.multiple_of(owner * B, B), B)
        grad = lax.dot_general(
            cps[...], wall[s], (((1,), (1,)), ((), ())), preferred_element_type=F32
        )
        tok[:, cols] = (grad - tok[:, cols].astype(F32) * inv_v[...]).astype(BF16)
        pltpu.make_async_copy(tok.at[:, cols], tg_o.at[:, cols], lsem.at[40 + s]).start()
        return 0

    def backward_done(s, _):
        owner = ((yl + s // 8) % 2) * 8 + ((z + (s // 2) % 4) % 4) * 2 + (c + s % 2) % 2
        cols = pl.ds(pl.multiple_of(owner * B, B), B)
        pltpu.make_async_copy(tok.at[:, cols], tg_o.at[:, cols], lsem.at[40 + s]).wait()
        return 0

    lax.fori_loop(0, 8, backward, 0)
    join_y(3)
    near[0] = near_free(0)
    lax.fori_loop(8, 16, backward, 0)
    spread_params(1)
    near[0] = near[0] + near_joined(0, far[0])

    for copy in near[2]:
        copy.wait_recv()
    gs[1, 0, pl.ds(K1, K2)] = (
        gs[1, 0, pl.ds(K1, K2)].astype(F32)
        + seg_rz0[2][...].astype(F32)
        + seg_rz1[2][...].astype(F32)
    ).astype(BF16)
    rz = send(gs.at[1, 0, pl.ds(K1, K2)], ryz, YP)

    for copy in near[1]:
        copy.wait_recv()
    low = (
        gs[0, 0, pl.ds(K1, K2)].astype(F32)
        + seg_rz0[1][...].astype(F32)
        + seg_rz1[1][...].astype(F32)
    )
    rys[0].wait_recv()
    high = gs[0, 0, pl.ds(0, K1)].astype(F32) + ry[0].astype(F32)
    for copy in near[0]:
        copy.wait_recv()
    high = high + seg_rz0[0][...].astype(F32) + seg_rz1[0][...].astype(F32)
    rz.wait_recv()
    low = low + ryz[...].astype(F32)
    total = jnp.concatenate([high, low], axis=0)
    gg_o[...] = jnp.sum(wt[...] * total, axis=0, keepdims=True)
    wgv[...] = jnp.transpose(total * gain_row)
    local(wgv, wgr_o.at[0])

    for p in range(PARTS):
        for dx in (1, 3, 2):
            npx[p, dx].wait_recv()
            npf[p, dx].wait_recv()
    for copy in started:
        copy.wait_send()
    lax.fori_loop(0, 16, backward_done, 0)
    done = {id(v) for v in [load_w, load_cot, load_pg, load_op, load_mo, *load_tok]}
    for copy in locals_:
        if id(copy) not in done:
            copy.wait()


def shards(tokens, norm_gain, value_weight, cotangent, pseudo_grad, outer_params, momentum):
    hbm = pl.BlockSpec(memory_space=pl.ANY)
    vmem = pl.BlockSpec(memory_space=pltpu.VMEM)
    out = jax.ShapeDtypeStruct
    return tuple(
        pl.pallas_call(
            kernel,
            out_shape=(
                out((T, K), BF16),
                out((T, D), BF16),
                out((1, B, K), F32),
                out((1, B), F32),
                out((ROWS, SHARE), F32),
                out((ROWS, SHARE), F32),
                out((ROWS, D), BF16),
            ),
            in_specs=[hbm, vmem, hbm, hbm, hbm, hbm, hbm],
            out_specs=(hbm, hbm, hbm, vmem, hbm, hbm, hbm),
            scratch_shapes=[
                pltpu.VMEM((T, D), BF16),
                pltpu.VMEM((8, T, B), BF16),
                pltpu.VMEM((N_FSDP, B, K), BF16),
                pltpu.VMEM((2, 4, K, B), BF16),
                pltpu.VMEM((4, K1, B), BF16),
                pltpu.VMEM((K2, B), BF16),
                pltpu.VMEM((3, K1 // 2, B), BF16),
                pltpu.VMEM((3, K1 // 2, B), BF16),
                pltpu.VMEM((3, K1, B), BF16),
                pltpu.VMEM((3, K1, B), BF16),
                pltpu.VMEM((B, K), BF16),
                pltpu.VMEM((K, B), F32),
                pltpu.VMEM((T, K), BF16),
                pltpu.VMEM((T, K), BF16),
                pltpu.VMEM((2, K, T), BF16),
                pltpu.VMEM((T, K), F32),
                pltpu.VMEM((T, 128), F32),
                pltpu.VMEM((T, 1), F32),
                pltpu.VMEM((B, K), F32),
                pltpu.VMEM((PARTS, 3, PR, 2 * SHARE), BF16),
                pltpu.VMEM((ROWS, 2 * SHARE), BF16),
                pltpu.VMEM((PARTS, PR, SHARE), BF16),
                pltpu.VMEM((PARTS, PR, SHARE), BF16),
                pltpu.VMEM((PARTS, PR, SHARE), F32),
                pltpu.VMEM((ROWS, SHARE), F32),
                pltpu.VMEM((ROWS, SHARE), F32),
                pltpu.VMEM((ROWS, SHARE), F32),
                pltpu.VMEM((ROWS, SHARE), F32),
                pltpu.VMEM((ROWS, SHARE), BF16),
                pltpu.VMEM((T, K), BF16),
                pltpu.SemaphoreType.DMA((N_COPIES,)),
                pltpu.SemaphoreType.DMA((N_COPIES,)),
                pltpu.SemaphoreType.DMA((64,)),
            ],
            compiler_params=pltpu.CompilerParams(
                collective_id=0, has_side_effects=True, vmem_limit_bytes=60 << 20
            ),
            name="window",
        )(tokens, norm_gain, value_weight, cotangent, pseudo_grad, outer_params, momentum)
    )


def solution(mesh):
    placed = (
        P(("group", "fsdp"), None),
        P("group", "fsdp"),
        P("group", "fsdp", None),
        P(("group", "fsdp"), None),
        P("group", "fsdp", None),
        P("fsdp", "group"),
        P("fsdp", "group"),
    )
    return jax.shard_map(
        shards,
        mesh=mesh,
        in_specs=placed,
        out_specs=(
            P(("group", "fsdp"), None),
            P(("group", "fsdp"), None),
            P("group", "fsdp", None),
            P("group", "fsdp"),
            P("fsdp", "group"),
            P("fsdp", "group"),
            P("fsdp", None),
        ),
        check_vma=False,
    )
```

time: 345 us -> 85.6 us (0.25)
  waiting for transfers between devices: 195 us -> 0 us
  blocking collectives: 76.7 us -> 0 us
  Pallas kernels: 0 us -> 69.8 us
  matrix products: 38.3 us -> 0 us
  other arithmetic: 17.2 us -> 0 us
  between operations: 14.4 us -> 0.66 us
  local copies, waits for them, and re-layouts: 3.2 us -> 14.3 us
    psum x1 -> x0, waiting for transfers between devices: 115 us -> none  [shards(): lax.psum(outer_terms.astype(jnp.bfloat16), 'group').astype(jnp.float32)]
    pallas_call x0 -> x1, Pallas kernels: none -> 69.8 us  [shards(): pl.pallas_call(kernel, out_shape=(out((T, K), BF16), out((T, D), BF16), o...]
    all_gather x2 -> x0, waiting for transfers between devices: 67.4 us -> none  [the longest x1 52.8 us: shards(): weight_piece = lax.all_gather(value_weight, 'fsdp', axis=1, tiled=True)]
    unnamed x1 -> x0, blocking collectives: 57.2 us -> none
    dot_general x3 -> x0, matrix products: 38.3 us -> none  [the longest x1 13.4 us: shards(): lax.dot_general(hidden, cotangent, (((0,), (0,)), ((), ())), preferred_el...]
    all_gather x1 -> x0, blocking collectives: 19.5 us -> none  [shards(): gain_piece = lax.all_gather(norm_gain, 'fsdp', axis=1, tiled=True)]
    convert_element_type x2 -> x0, other arithmetic: 12 us -> none  [the longest x1 9.46 us: shards(): token_grad.astype(jnp.bfloat16)]
    unnamed x13 -> x17, local copies, waits for them, and re-layouts: 3.2 us -> 14.3 us
  transfers between devices with their start and end apart: 4 -> 0, of which waited for: 4 -> 0; matrix products, arithmetic and copies ran while one was open for 16% -> 0% of each run, Pallas kernels for 0% -> 0%
where the time goes in v1:
time: 85.6 us; the launch traced here: 84.7 us
  Pallas kernels  69.8 us (82%)
  local copies, waits for them, and re-layouts  14.3 us (17%)
    pallas_call x1, Pallas kernels, shards(): pl.pallas_call(kernel, out_shape=(out((T, K), BF16), out((T, D), BF16), o...  69.8 us
    unnamed x17, local copies, waits for them, and re-layouts  14.3 us

profile of v1, /device:TPU:0, one launch (start us, length us, event | category | flops | bytes accessed | tf_op | source)
XLA Modules:
  0.0 84.7 jit_solution(8051985278252074070)
XLA Ops:
  0.6 69.8 %window.1 = (bf16[512,512]{1,0:T(8,128)(2,1)}, bf16[512,8192]{1,0:T(8,128)(2,1)}, f32[1,512,512]{2,1,0:T(8,128)}, f32[1,512]{1,0:T(1,128)}, f32[128,1024]{1,0:T(...) custom-call(bf16[512,8192]{1,0:T(8,128)(2,1)} %tok_hbm.1, bf16[1,512]{1,0:T(2,128)(2,1)} %gain_ref.1, ...), custom_call_target="tpu_custom_call" | custom-call | tf_op jit(solution)/shard_map/window/pallas_call | solution.py:419
  70.4 1.9 %copy.21 = bf16[512,512]{1,0:T(8,128)(2,1)} copy(bf16[512,512]{1,0:T(8,128)(2,1)} %get-tuple-element.14) | data formatting | bytes 1048576
  72.3 0.0 copy-start.1
  72.3 0.0 copy-start.4
  72.3 0.0 copy-start.3
  72.3 0.0 copy-start.2
  72.3 0.0 copy-start
  72.3 7.9 %copy.22 = bf16[512,8192]{1,0:T(8,128)(2,1)} copy(bf16[512,8192]{1,0:T(8,128)(2,1)} %get-tuple-element.15) | data formatting | bytes 16777216
  80.2 0.0 copy-done.1
  80.2 1.0 %copy.23 = f32[1,512,512]{2,1,0:T(8,128)} copy(f32[1,512,512]{2,1,0:T(8,128)S(1)} %copy-done.1) | data formatting | bytes 2097152
  81.2 0.0 copy-done.4
  81.2 0.6 copy.24
  81.8 0.0 copy-done.3
  81.8 0.8 copy.25
  82.6 0.0 copy-done.2
  82.6 0.8 copy.26
  83.4 0.0 copy-done
  83.4 1.3 %copy.27 = bf16[128,8192]{1,0:T(8,128)(2,1)} copy(bf16[128,8192]{1,0:T(8,128)(2,1)S(1)} %copy-done) | data formatting | bytes 4194304
Async XLA Ops:
  72.3 7.9 %copy-start.1 = (f32[1,512,512]{2,1,0:T(8,128)S(1)}, f32[1,512,512]{2,1,0:T(8,128)}, u32[]{:S(2)}) copy-start(f32[1,512,512]{2,1,0:T(8,128)} %get-tuple-element.16) | copy-start | bytes 3145732
  72.3 8.9 %copy-start.4 = (f32[1,512]{1,0:T(1,128)S(1)}, f32[1,512]{1,0:T(1,128)}, u32[]{:S(2)}) copy-start(f32[1,512]{1,0:T(1,128)} %get-tuple-element.17) | copy-start | bytes 6148
  72.3 9.5 %copy-start.3 = (f32[128,1024]{1,0:T(8,128)S(1)}, f32[128,1024]{1,0:T(8,128)}, u32[]{:S(2)}) copy-start(f32[128,1024]{1,0:T(8,128)} %get-tuple-element.18) | copy-start | bytes 1572868
  72.3 10.3 %copy-start.2 = (f32[128,1024]{1,0:T(8,128)S(1)}, f32[128,1024]{1,0:T(8,128)}, u32[]{:S(2)}) copy-start(f32[128,1024]{1,0:T(8,128)} %get-tuple-element.19) | copy-start | bytes 1572868
  72.3 11.1 %copy-start = (bf16[128,8192]{1,0:T(8,128)(2,1)S(1)}, bf16[128,8192]{1,0:T(8,128)(2,1)}, u32[]{:S(2)}) copy-start(bf16[128,8192]{1,0:T(8,128)(2,1)} %get-tuple-element.20) | copy-start | bytes 6291460

commit v2 on v1

--- a/solution.py
+++ b/solution.py
@@ -24,8 +24,10 @@
 SHARE = 1024
 PARTS = 2
 PR = ROWS // PARTS
-K1 = 320
+K1 = 352
 K2 = K - K1
+M1 = 176
+M2 = 96
 CHUNK = 1024
 N_CHUNK = D // CHUNK
 N_COPIES = 96
@@ -33,10 +35,10 @@
 
 def kernel(
     tok_hbm, gain_ref, w_hbm, cot_hbm, pg_hbm, op_hbm, mo_hbm,
-    val_o, tg_o, wgr_o, gg_o, ng_o, nm_o, np_o,
-    tok, sibtok, wall, gs, ry, ryz, rh0, rh1, rz0, rz1,
-    w_v, wt, cot_v, cps, cott, acc, sq, inv_v, wgv,
-    px, pown, pys, pyr, psum, op_v, mo_v, ng_v, nm_v, np_v, val_v,
+    val_v, tok, sum_v, rzp, rzm, ryz, wt, ng_v, nm_v, np_v,
+    sibtok, wall, gs, ry, rh0, rh1, rz0, rz1,
+    w_v, cot_v, cps, cott, acc, sq, inv_v,
+    px, pown, pys, pyr, psum, op_v, mo_v,
     ssem, rsem, lsem,
 ):
     group = lax.axis_index("group")
@@ -170,41 +172,46 @@
         other = jnp.dot(cott[1], sibtok[dy * 4 + dz], preferred_element_type=F32)
         gs[dy, dz] = (own + other).astype(BF16)
 
-    SEG = {0: (0, 0, K1), 1: (0, K1, K2), 2: (1, K1, K2)}
-    seg_rh0 = {0: rh0.at[0, :K1 // 2], 1: rh0.at[1, :K2 // 2], 2: rh0.at[2, :K2 // 2]}
-    seg_rh1 = {0: rh1.at[0, :K1 // 2], 1: rh1.at[1, :K2 // 2], 2: rh1.at[2, :K2 // 2]}
-    seg_rz0 = {0: rz0.at[0, :K1], 1: rz0.at[1, :K2], 2: rz0.at[2, :K2]}
-    seg_rz1 = {0: rz1.at[0, :K1], 1: rz1.at[1, :K2], 2: rz1.at[2, :K2]}
+    SEG = {0: (0, 0, K1, M1), 1: (0, K1, K2, M2), 2: (1, K1, K2, M2)}
+    seg_rh0 = {0: rh0.at[0, :M1], 1: rh0.at[1, :M2], 2: rh0.at[2, :M2]}
+    seg_rh1 = {0: rh1.at[0, :K1 - M1], 1: rh1.at[1, :K2 - M2], 2: rh1.at[2, :K2 - M2]}
+    seg_rz0 = {0: rzp, 1: rz0.at[0], 2: rz0.at[1]}
+    seg_rz1 = {0: rzm, 1: rz1.at[0], 2: rz1.at[1]}
 
     def far_halves(g):
-        dy, r0, n = SEG[g]
-        m = n // 2
+        dy, r0, n, m = SEG[g]
         return (
             send(gs.at[dy, 2, pl.ds(r0, m)], seg_rh0[g], ZP),
-            send(gs.at[dy, 2, pl.ds(r0 + m, m)], seg_rh1[g], ZM),
+            send(gs.at[dy, 2, pl.ds(r0 + m, n - m)], seg_rh1[g], ZM),
         )
 
     def add_into(ref, other):
         ref[...] = (ref[...].astype(F32) + other[...].astype(F32)).astype(BF16)
 
-    def near_free(g):
-        dy, r0, n = SEG[g]
-        m = n // 2
-        return [
-            send(gs.at[dy, 1, pl.ds(r0 + m, m)], seg_rz0[g].at[pl.ds(m, m)], ZP),
-            send(gs.at[dy, 3, pl.ds(r0, m)], seg_rz1[g].at[pl.ds(0, m)], ZM),
-        ]
-
-    def near_joined(g, far):
-        dy, r0, n = SEG[g]
-        m = n // 2
-        far[0].wait_recv()
-        add_into(gs.at[dy, 1, pl.ds(r0, m)], seg_rh0[g])
-        a = send(gs.at[dy, 1, pl.ds(r0, m)], seg_rz0[g].at[pl.ds(0, m)], ZP)
-        far[1].wait_recv()
-        add_into(gs.at[dy, 3, pl.ds(r0 + m, m)], seg_rh1[g])
-        b = send(gs.at[dy, 3, pl.ds(r0 + m, m)], seg_rz1[g].at[pl.ds(m, m)], ZM)
-        return [a, b]
+    near = {0: [], 1: [], 2: []}
+
+    def near_free(g, dz):
+        dy, r0, n, m = SEG[g]
+        if dz == 1:
+            copy = send(
+                gs.at[dy, 1, pl.ds(r0 + m, n - m)], seg_rz0[g].at[pl.ds(m, n - m)], ZP
+            )
+        else:
+            copy = send(gs.at[dy, 3, pl.ds(r0, m)], seg_rz1[g].at[pl.ds(0, m)], ZM)
+        near[g].append(copy)
+
+    def near_joined(g, dz):
+        dy, r0, n, m = SEG[g]
+        far[g][0 if dz == 1 else 1].wait_recv()
+        if dz == 1:
+            add_into(gs.at[dy, 1, pl.ds(r0, m)], seg_rh0[g])
+            copy = send(gs.at[dy, 1, pl.ds(r0, m)], seg_rz0[g].at[pl.ds(0, m)], ZP)
+        else:
+            add_into(gs.at[dy, 3, pl.ds(r0 + m, n - m)], seg_rh1[g])
+            copy = send(
+                gs.at[dy, 3, pl.ds(r0 + m, n - m)], seg_rz1[g].at[pl.ds(m, n - m)], ZM
+            )
+        near[g].append(copy)
 
     def across_y(dz):
         return send(gs.at[1, dz, pl.ds(0, K1)], ry.at[dz], YP)
@@ -287,18 +294,15 @@
         new_global = op_v[rr] - outer_rate * (average + momentum_decay * new_momentum)
         nm_v[rr] = new_momentum
         ng_v[rr] = new_global
-        np_v[rr] = new_global.astype(BF16)
-        place = np_o.at[rr, share_cols(0)]
-        npy[p] = send(np_v.at[rr], place, Y2)
+        np_v[rr, share_cols(0)] = new_global.astype(BF16)
+        place = np_v.at[rr, share_cols(0)]
+        npy[p] = send(place, place, Y2)
         for dx in (1, 3, 2):
-            npx[p, dx] = send(np_v.at[rr], place, XS[dx])
-        local(np_v.at[rr], place)
-        local(nm_v.at[rr], nm_o.at[rr])
-        local(ng_v.at[rr], ng_o.at[rr])
+            npx[p, dx] = send(place, place, XS[dx])
 
     def spread_params(p):
         npy[p].wait_recv()
-        place = np_o.at[rows(p), share_cols(1)]
+        place = np_v.at[rows(p), share_cols(1)]
         for dx in (1, 3, 2):
             npf[p, dx] = send(place, place, XS[dx])
 
@@ -323,10 +327,15 @@
     afar[1] = far_forward(1)
     rest_of_near(1)
     far[0] = far_halves(0)
-    near = {g: near_free(g) + near_joined(g, far[g]) for g in (2, 1)}
+    for g in (2, 1):
+        near_free(g, 1)
+        near_free(g, 3)
+        near_joined(g, 1)
+        near_joined(g, 3)
     forward(1, 1, 0)
     forward(1, 3, 0)
     join_y(1)
+    near_free(0, 1)
     rest_of_far(0)
     outer_step(1)
     rys[0] = across_y(0)
@@ -340,13 +349,6 @@
     sib[1, 2].wait_recv()
     forward(1, 2, 1)
 
-    inv = inv_v[...]
-    acc_v = acc[...]
-    val_v[...] = (acc_v * inv).astype(BF16)
-    local(val_v, val_o)
-    inner = jnp.sum(cot_v[...].astype(F32) * acc_v, axis=1, keepdims=True)
-    inv_v[...] = inv * inv * inv * inner * (1.0 / D)
-
     def backward(s, _):
         owner = ((yl + s // 8) % 2) * 8 + ((z + (s // 2) % 4) % 4) * 2 + (c + s % 2) % 2
         cols = pl.ds(pl.multiple_of(owner * B, B), B)
@@ -354,21 +356,20 @@
             cps[...], wall[s], (((1,), (1,)), ((), ())), preferred_element_type=F32
         )
         tok[:, cols] = (grad - tok[:, cols].astype(F32) * inv_v[...]).astype(BF16)
-        pltpu.make_async_copy(tok.at[:, cols], tg_o.at[:, cols], lsem.at[40 + s]).start()
         return 0
 
-    def backward_done(s, _):
-        owner = ((yl + s // 8) % 2) * 8 + ((z + (s // 2) % 4) % 4) * 2 + (c + s % 2) % 2
-        cols = pl.ds(pl.multiple_of(owner * B, B), B)
-        pltpu.make_async_copy(tok.at[:, cols], tg_o.at[:, cols], lsem.at[40 + s]).wait()
-        return 0
+    join_y(3)
+    near_free(0, 3)
+    near_joined(0, 1)
+    near_joined(0, 3)
+    inv = inv_v[...]
+    acc_v = acc[...]
+    val_v[...] = (acc_v * inv).astype(BF16)
+    inner = jnp.sum(cot_v[...].astype(F32) * acc_v, axis=1, keepdims=True)
+    inv_v[...] = inv * inv * inv * inner * (1.0 / D)
 
     lax.fori_loop(0, 8, backward, 0)
-    join_y(3)
-    near[0] = near_free(0)
-    lax.fori_loop(8, 16, backward, 0)
     spread_params(1)
-    near[0] = near[0] + near_joined(0, far[0])
 
     for copy in near[2]:
         copy.wait_recv()
@@ -378,46 +379,109 @@
         + seg_rz1[2][...].astype(F32)
     ).astype(BF16)
     rz = send(gs.at[1, 0, pl.ds(K1, K2)], ryz, YP)
+    lax.fori_loop(8, 16, backward, 0)
 
     for copy in near[1]:
         copy.wait_recv()
-    low = (
-        gs[0, 0, pl.ds(K1, K2)].astype(F32)
-        + seg_rz0[1][...].astype(F32)
-        + seg_rz1[1][...].astype(F32)
+    low = pl.ds(K1, K2)
+    sum_v[low] = (
+        gs[0, 0, low].astype(F32) + seg_rz0[1][...].astype(F32) + seg_rz1[1][...].astype(F32)
     )
     rys[0].wait_recv()
-    high = gs[0, 0, pl.ds(0, K1)].astype(F32) + ry[0].astype(F32)
-    for copy in near[0]:
-        copy.wait_recv()
-    high = high + seg_rz0[0][...].astype(F32) + seg_rz1[0][...].astype(F32)
-    rz.wait_recv()
-    low = low + ryz[...].astype(F32)
-    total = jnp.concatenate([high, low], axis=0)
-    gg_o[...] = jnp.sum(wt[...] * total, axis=0, keepdims=True)
-    wgv[...] = jnp.transpose(total * gain_row)
-    local(wgv, wgr_o.at[0])
-
+    high = pl.ds(0, K1)
+    sum_v[high] = gs[0, 0, high].astype(F32) + ry[0].astype(F32)
     for p in range(PARTS):
         for dx in (1, 3, 2):
             npx[p, dx].wait_recv()
             npf[p, dx].wait_recv()
+    for copy in near[0]:
+        copy.wait_recv()
+    rz.wait_recv()
     for copy in started:
         copy.wait_send()
-    lax.fori_loop(0, 16, backward_done, 0)
-    done = {id(v) for v in [load_w, load_cot, load_pg, load_op, load_mo, *load_tok]}
-    for copy in locals_:
-        if id(copy) not in done:
-            copy.wait()
+
+
+def finish(
+    gain_ref, val_v, tg_v, sum_v, rzp, rzm, ryz, wt, ng_v, nm_v, np_v,
+    val_o, tg_o, wgr_o, gg_o, ng_o, nm_o, np_o, wgv, ggv, sems,
+):
+    copies = [
+        pltpu.make_async_copy(src, dst, sems.at[n])
+        for n, (src, dst) in enumerate(
+            [(tg_v, tg_o), (np_v, np_o), (val_v, val_o), (ng_v, ng_o), (nm_v, nm_o)]
+        )
+    ]
+    for copy in copies:
+        copy.start()
+    high = sum_v[:K1] + rzp[...].astype(F32) + rzm[...].astype(F32)
+    low = sum_v[K1:] + ryz[...].astype(F32)
+    total = jnp.concatenate([high, low], axis=0)
+    wgv[...] = jnp.transpose(total * gain_ref[...].astype(F32))
+    copies.append(pltpu.make_async_copy(wgv, wgr_o.at[0], sems.at[5]))
+    copies[-1].start()
+    ggv[...] = jnp.sum(wt[...] * total, axis=0, keepdims=True)
+    copies.append(pltpu.make_async_copy(ggv, gg_o, sems.at[6]))
+    copies[-1].start()
+    for copy in copies:
+        copy.wait()
 
 
 def shards(tokens, norm_gain, value_weight, cotangent, pseudo_grad, outer_params, momentum):
     hbm = pl.BlockSpec(memory_space=pl.ANY)
     vmem = pl.BlockSpec(memory_space=pltpu.VMEM)
     out = jax.ShapeDtypeStruct
+    held = pl.pallas_call(
+        kernel,
+        out_shape=(
+            pltpu.VMEM((T, K), BF16),
+            pltpu.VMEM((T, D), BF16),
+            pltpu.VMEM((K, B), F32),
+            pltpu.VMEM((K1, B), BF16),
+            pltpu.VMEM((K1, B), BF16),
+            pltpu.VMEM((K2, B), BF16),
+            pltpu.VMEM((K, B), F32),
+            pltpu.VMEM((ROWS, SHARE), F32),
+            pltpu.VMEM((ROWS, SHARE), F32),
+            pltpu.VMEM((ROWS, D), BF16),
+        ),
+        in_specs=[hbm, vmem, hbm, hbm, hbm, hbm, hbm],
+        out_specs=(vmem,) * 10,
+        scratch_shapes=[
+            pltpu.VMEM((8, T, B), BF16),
+            pltpu.VMEM((N_FSDP, B, K), BF16),
+            pltpu.VMEM((2, 4, K, B), BF16),
+            pltpu.VMEM((4, K1, B), BF16),
+            pltpu.VMEM((3, M1, B), BF16),
+            pltpu.VMEM((3, M1, B), BF16),
+            pltpu.VMEM((2, K2, B), BF16),
+            pltpu.VMEM((2, K2, B), BF16),
+            pltpu.VMEM((B, K), BF16),
+            pltpu.VMEM((T, K), BF16),
+            pltpu.VMEM((T, K), BF16),
+            pltpu.VMEM((2, K, T), BF16),
+            pltpu.VMEM((T, K), F32),
+            pltpu.VMEM((T, 128), F32),
+            pltpu.VMEM((T, 1), F32),
+            pltpu.VMEM((PARTS, 3, PR, 2 * SHARE), BF16),
+            pltpu.VMEM((ROWS, 2 * SHARE), BF16),
+            pltpu.VMEM((PARTS, PR, SHARE), BF16),
+            pltpu.VMEM((PARTS, PR, SHARE), BF16),
+            pltpu.VMEM((PARTS, PR, SHARE), F32),
+            pltpu.VMEM((ROWS, SHARE), F32),
+            pltpu.VMEM((ROWS, SHARE), F32),
+            pltpu.SemaphoreType.DMA((N_COPIES,)),
+            pltpu.SemaphoreType.DMA((N_COPIES,)),
+            pltpu.SemaphoreType.DMA((16,)),
+        ],
+        compiler_params=pltpu.CompilerParams(
+            collective_id=0, has_side_effects=True, vmem_limit_bytes=40 << 20
+        ),
+        name="window",
+    )(tokens, norm_gain, value_weight, cotangent, pseudo_grad, outer_params, momentum)
+    held = [pltpu.with_memory_space_constraint(v, pltpu.VMEM) for v in held]
     return tuple(
         pl.pallas_call(
-            kernel,
+            finish,
             out_shape=(
                 out((T, K), BF16),
                 out((T, D), BF16),
@@ -427,48 +491,16 @@
                 out((ROWS, SHARE), F32),
                 out((ROWS, D), BF16),
             ),
-            in_specs=[hbm, vmem, hbm, hbm, hbm, hbm, hbm],
-            out_specs=(hbm, hbm, hbm, vmem, hbm, hbm, hbm),
+            in_specs=[vmem] * 11,
+            out_specs=(hbm,) * 7,
             scratch_shapes=[
-                pltpu.VMEM((T, D), BF16),
-                pltpu.VMEM((8, T, B), BF16),
-                pltpu.VMEM((N_FSDP, B, K), BF16),
-                pltpu.VMEM((2, 4, K, B), BF16),
-                pltpu.VMEM((4, K1, B), BF16),
-                pltpu.VMEM((K2, B), BF16),
-                pltpu.VMEM((3, K1 // 2, B), BF16),
-                pltpu.VMEM((3, K1 // 2, B), BF16),
-                pltpu.VMEM((3, K1, B), BF16),
-                pltpu.VMEM((3, K1, B), BF16),
-                pltpu.VMEM((B, K), BF16),
-                pltpu.VMEM((K, B), F32),
-                pltpu.VMEM((T, K), BF16),
-                pltpu.VMEM((T, K), BF16),
-                pltpu.VMEM((2, K, T), BF16),
-                pltpu.VMEM((T, K), F32),
-                pltpu.VMEM((T, 128), F32),
-                pltpu.VMEM((T, 1), F32),
                 pltpu.VMEM((B, K), F32),
-                pltpu.VMEM((PARTS, 3, PR, 2 * SHARE), BF16),
-                pltpu.VMEM((ROWS, 2 * SHARE), BF16),
-                pltpu.VMEM((PARTS, PR, SHARE), BF16),
-                pltpu.VMEM((PARTS, PR, SHARE), BF16),
-                pltpu.VMEM((PARTS, PR, SHARE), F32),
-                pltpu.VMEM((ROWS, SHARE), F32),
-                pltpu.VMEM((ROWS, SHARE), F32),
-                pltpu.VMEM((ROWS, SHARE), F32),
-                pltpu.VMEM((ROWS, SHARE), F32),
-                pltpu.VMEM((ROWS, SHARE), BF16),
-                pltpu.VMEM((T, K), BF16),
-                pltpu.SemaphoreType.DMA((N_COPIES,)),
-                pltpu.SemaphoreType.DMA((N_COPIES,)),
-                pltpu.SemaphoreType.DMA((64,)),
+                pltpu.VMEM((1, B), F32),
+                pltpu.SemaphoreType.DMA((8,)),
             ],
-            compiler_params=pltpu.CompilerParams(
-                collective_id=0, has_side_effects=True, vmem_limit_bytes=60 << 20
-            ),
-            name="window",
-        )(tokens, norm_gain, value_weight, cotangent, pseudo_grad, outer_params, momentum)
+            compiler_params=pltpu.CompilerParams(vmem_limit_bytes=16 << 20),
+            name="finish",
+        )(norm_gain, *held)
     )
 
 

time: 85.6 us -> 72.7 us (0.85)
  local copies, waits for them, and re-layouts: 14.3 us -> 0.01 us
  Pallas kernels: 69.8 us -> 71.9 us
    unnamed x17 -> x2, local copies, waits for them, and re-layouts: 14.3 us -> 0.01 us
    pallas_call x1 -> x2, Pallas kernels: 69.8 us -> 71.9 us  [the longest x1 67 us: shards(): pl.pallas_call(kernel, out_shape=(pltpu.VMEM((T, K), BF16), pltpu.VMEM((T...]
where the time goes in v2:
time: 72.7 us; the launch traced here: 72.6 us
  Pallas kernels  71.9 us (99%)
    pallas_call x1, Pallas kernels, shards(): pl.pallas_call(kernel, out_shape=(pltpu.VMEM((T, K), BF16), pltpu.VMEM((T...  67 us
    pallas_call x1, Pallas kernels, shards(): pl.pallas_call(finish, out_shape=(out((T, K), BF16), out((T, D), BF16), o...  4.91 us

profile of v2, /device:TPU:0, one launch (start us, length us, event | category | flops | bytes accessed | tf_op | source)
XLA Modules:
  0.0 72.6 jit_solution(12353937205924723517)
XLA Ops:
  0.6 0.0 copy-start
  0.6 67.0 %window.1 = (bf16[512,512]{1,0:T(8,128)(2,1)S(1)}, bf16[512,8192]{1,0:T(8,128)(2,1)S(1)}, f32[512,512]{1,0:T(8,128)S(1)}, bf16[352,512]{1,0:T(8,128)(2,1)S(1)}, ...) custom-call(bf16[512,8192]{1,0:T(8,128)(2,1)} %tok_hbm.1, ...), custom_call_target="tpu_custom_call" | custom-call | tf_op jit(solution)/shard_map/window/pallas_call | solution.py:433
  67.6 0.0 copy-done
  67.7 4.9 %finish.1 = (bf16[512,512]{1,0:T(8,128)(2,1)}, bf16[512,8192]{1,0:T(8,128)(2,1)}, f32[1,512,512]{2,1,0:T(8,128)}, f32[1,512]{1,0:T(1,128)}, f32[128,1024]{1,0:T(...) custom-call(bf16[1,512]{1,0:T(2,128)(2,1)S(1)} %copy-done, bf16[512,512]{1,0:T(8,128)(2,1)S(1)} %get-tuple-element.17.val_v, ...), custom_call_target="tpu_custom_call" | custom-call | tf_op jit(solution)/shard_map/finish/pallas_call | solution.py:483
Async XLA Ops:
  0.6 67.0 %copy-start = (bf16[1,512]{1,0:T(2,128)(2,1)S(1)}, bf16[1,512]{1,0:T(2,128)(2,1)}, u32[]{:S(2)}) copy-start(bf16[1,512]{1,0:T(2,128)(2,1)} %gain_ref.3) | copy-start | bytes 3076

commit v3 on v2

--- a/solution.py
+++ b/solution.py
@@ -34,8 +34,8 @@
 
 
 def kernel(
-    tok_hbm, gain_ref, w_hbm, cot_hbm, pg_hbm, op_hbm, mo_hbm,
-    val_v, tok, sum_v, rzp, rzm, ryz, wt, ng_v, nm_v, np_v,
+    tok_hbm, gain_hbm, w_hbm, cot_hbm, pg_hbm, op_hbm, mo_hbm,
+    val_v, tok, sum_v, ryo, rzp, rzm, ryz, wt, ng_v, nm_v, np_v, gain_v,
     sibtok, wall, gs, ry, rh0, rh1, rz0, rz1,
     w_v, cot_v, cps, cott, acc, sq, inv_v,
     px, pown, pys, pyr, psum, op_v, mo_v,
@@ -81,7 +81,13 @@
         locals_.append(copy)
         return copy
 
+    barrier = pltpu.get_barrier_semaphore()
+    partners = [SIB, YP, ZP, ZM, Y2, XS[1], XS[3], XS[2]]
+    for to in partners:
+        pl.semaphore_signal(barrier, inc=1, device_id=to, device_id_type=pl.DeviceIdType.MESH)
+
     load_w = local(w_hbm.at[0], w_v)
+    load_gain = local(gain_hbm, gain_v)
     load_tok = [
         local(tok_hbm.at[:, pl.ds(i * CHUNK, CHUNK)], tok.at[:, pl.ds(i * CHUNK, CHUNK)])
         for i in range(N_CHUNK)
@@ -92,13 +98,9 @@
     load_op = local(op_hbm, op_v)
     load_mo = local(mo_hbm, mo_v)
 
-    barrier = pltpu.get_barrier_semaphore()
-    partners = [SIB, YP, ZP, ZM, Y2, XS[1], XS[3], XS[2]]
-    for to in partners:
-        pl.semaphore_signal(barrier, inc=1, device_id=to, device_id_type=pl.DeviceIdType.MESH)
-
+    load_gain.wait()
     load_w.wait()
-    gain_row = gain_ref[...].astype(F32)
+    gain_row = gain_v[...].astype(F32)
     gain_col = jnp.transpose(jnp.broadcast_to(gain_row, (128, B)))
     wall[0] = (w_v[...].astype(F32) * jnp.concatenate([gain_col] * 4, axis=1)).astype(BF16)
 
@@ -214,11 +216,12 @@
         near[g].append(copy)
 
     def across_y(dz):
-        return send(gs.at[1, dz, pl.ds(0, K1)], ry.at[dz], YP)
+        there = ryo if dz == 0 else ry.at[dz - 1]
+        return send(gs.at[1, dz, pl.ds(0, K1)], there, YP)
 
     def join_y(dz):
         rys[dz].wait_recv()
-        add_into(gs.at[0, dz, pl.ds(0, K1)], ry.at[dz])
+        add_into(gs.at[0, dz, pl.ds(0, K1)], ry.at[dz - 1])
 
     rys, far = {}, {}
     ct.wait_recv()
@@ -381,28 +384,33 @@
     rz = send(gs.at[1, 0, pl.ds(K1, K2)], ryz, YP)
     lax.fori_loop(8, 16, backward, 0)
 
+    high, low = pl.ds(0, K1), pl.ds(K1, K2)
+    sum_v[high] = gs[0, 0, high].astype(F32)
     for copy in near[1]:
         copy.wait_recv()
-    low = pl.ds(K1, K2)
     sum_v[low] = (
         gs[0, 0, low].astype(F32) + seg_rz0[1][...].astype(F32) + seg_rz1[1][...].astype(F32)
     )
-    rys[0].wait_recv()
-    high = pl.ds(0, K1)
-    sum_v[high] = gs[0, 0, high].astype(F32) + ry[0].astype(F32)
     for p in range(PARTS):
         for dx in (1, 3, 2):
             npx[p, dx].wait_recv()
+    late = [rz, rys[0], *near[0], *(npf[1, dx] for dx in (1, 3, 2))]
+    for copy in started:
+        if not any(copy is other for other in late):
+            copy.wait_send()
+    for p in range(PARTS):
+        for dx in (1, 3, 2):
             npf[p, dx].wait_recv()
-    for copy in near[0]:
+    for copy in late[2:]:
+        copy.wait_send()
+    for copy in [*near[0], rys[0], rz]:
         copy.wait_recv()
-    rz.wait_recv()
-    for copy in started:
-        copy.wait_send()
+    rys[0].wait_send()
+    rz.wait_send()
 
 
 def finish(
-    gain_ref, val_v, tg_v, sum_v, rzp, rzm, ryz, wt, ng_v, nm_v, np_v,
+    val_v, tg_v, sum_v, ryo, rzp, rzm, ryz, wt, ng_v, nm_v, np_v, gain_v,
     val_o, tg_o, wgr_o, gg_o, ng_o, nm_o, np_o, wgv, ggv, sems,
 ):
     copies = [
@@ -413,10 +421,10 @@
     ]
     for copy in copies:
         copy.start()
-    high = sum_v[:K1] + rzp[...].astype(F32) + rzm[...].astype(F32)
+    high = sum_v[:K1] + ryo[...].astype(F32) + rzp[...].astype(F32) + rzm[...].astype(F32)
     low = sum_v[K1:] + ryz[...].astype(F32)
     total = jnp.concatenate([high, low], axis=0)
-    wgv[...] = jnp.transpose(total * gain_ref[...].astype(F32))
+    wgv[...] = jnp.transpose(total * gain_v[...].astype(F32))
     copies.append(pltpu.make_async_copy(wgv, wgr_o.at[0], sems.at[5]))
     copies[-1].start()
     ggv[...] = jnp.sum(wt[...] * total, axis=0, keepdims=True)
@@ -438,19 +446,21 @@
             pltpu.VMEM((K, B), F32),
             pltpu.VMEM((K1, B), BF16),
             pltpu.VMEM((K1, B), BF16),
+            pltpu.VMEM((K1, B), BF16),
             pltpu.VMEM((K2, B), BF16),
             pltpu.VMEM((K, B), F32),
             pltpu.VMEM((ROWS, SHARE), F32),
             pltpu.VMEM((ROWS, SHARE), F32),
             pltpu.VMEM((ROWS, D), BF16),
+            pltpu.VMEM((1, B), BF16),
         ),
-        in_specs=[hbm, vmem, hbm, hbm, hbm, hbm, hbm],
-        out_specs=(vmem,) * 10,
+        in_specs=[hbm] * 7,
+        out_specs=(vmem,) * 12,
         scratch_shapes=[
             pltpu.VMEM((8, T, B), BF16),
             pltpu.VMEM((N_FSDP, B, K), BF16),
             pltpu.VMEM((2, 4, K, B), BF16),
-            pltpu.VMEM((4, K1, B), BF16),
+            pltpu.VMEM((3, K1, B), BF16),
             pltpu.VMEM((3, M1, B), BF16),
             pltpu.VMEM((3, M1, B), BF16),
             pltpu.VMEM((2, K2, B), BF16),
@@ -491,7 +501,7 @@
                 out((ROWS, SHARE), F32),
                 out((ROWS, D), BF16),
             ),
-            in_specs=[vmem] * 11,
+            in_specs=[vmem] * 12,
             out_specs=(hbm,) * 7,
             scratch_shapes=[
                 pltpu.VMEM((B, K), F32),
@@ -500,7 +510,7 @@
             ],
             compiler_params=pltpu.CompilerParams(vmem_limit_bytes=16 << 20),
             name="finish",
-        )(norm_gain, *held)
+        )(*held)
     )
 
 

time: 72.7 us -> 72 us (level)
  no operation moved by 1% of the time
where the time goes in v3:
time: 72 us; the launch traced here: 71.8 us
  Pallas kernels  71.2 us (99%)
    pallas_call x1, Pallas kernels, shards(): pl.pallas_call(kernel, out_shape=(pltpu.VMEM((T, K), BF16), pltpu.VMEM((T...  66.3 us
    pallas_call x1, Pallas kernels, shards(): pl.pallas_call(finish, out_shape=(out((T, K), BF16), out((T, D), BF16), o...  4.91 us

profile of v3, /device:TPU:0, one launch (start us, length us, event | category | flops | bytes accessed | tf_op | source)
XLA Modules:
  0.0 71.8 jit_solution(8876940641906581446)
XLA Ops:
  0.6 66.3 %window.1 = (bf16[512,512]{1,0:T(8,128)(2,1)S(1)}, bf16[512,8192]{1,0:T(8,128)(2,1)S(1)}, f32[512,512]{1,0:T(8,128)S(1)}, bf16[352,512]{1,0:T(8,128)(2,1)S(1)}, ...) custom-call(bf16[512,8192]{1,0:T(8,128)(2,1)} %tok_hbm.1, ...), custom_call_target="tpu_custom_call" | custom-call | tf_op jit(solution)/shard_map/window/pallas_call | solution.py:441
  66.9 4.9 %finish.1 = (bf16[512,512]{1,0:T(8,128)(2,1)}, bf16[512,8192]{1,0:T(8,128)(2,1)}, f32[1,512,512]{2,1,0:T(8,128)}, f32[1,512]{1,0:T(1,128)}, f32[128,1024]{1,0:T(...) custom-call(bf16[512,512]{1,0:T(8,128)(2,1)S(1)} %get-tuple-element.19.val_v, ...), custom_call_target="tpu_custom_call" | custom-call | tf_op jit(solution)/shard_map/finish/pallas_call | solution.py:493

commit v4 on v3

--- a/solution.py
+++ b/solution.py
@@ -28,6 +28,7 @@
 K2 = K - K1
 M1 = 176
 M2 = 96
+SHIFT = 32
 CHUNK = 1024
 N_CHUNK = D // CHUNK
 N_COPIES = 96
@@ -65,14 +66,18 @@
     started = []
     locals_ = []
 
-    def send(src, dst, to):
+    def send(src, dst, to, when=None, land=None):
         n = len(started)
         copy = pltpu.make_async_remote_copy(
-            src_ref=src, dst_ref=dst, send_sem=ssem.at[n], recv_sem=rsem.at[n],
+            src_ref=src, dst_ref=dst, send_sem=ssem.at[n],
+            recv_sem=rsem.at[n if land is None else land],
             device_id=to, device_id_type=pl.DeviceIdType.MESH,
         )
-        copy.start()
-        started.append(copy)
+        if when is None:
+            copy.start()
+        else:
+            pl.when(when)(copy.start)
+        started.append((copy, when))
         return copy
 
     def local(src, dst):
@@ -239,17 +244,29 @@
             tok[:, pl.ds(col(dy, dz, dc), B)], wall[slot(dy, dz, dc)], preferred_element_type=F32
         )
 
+    def part(dy, dz, r0, r1):
+        return wall.at[slot(dy, dz, 0), pl.ds(r0, r1 - r0)]
+
+    lo, hi = H - SHIFT, H + SHIFT
+    middle = {}
+
     def far_forward(dy):
         az[dy]["m", 0].wait_recv()
-        a = send(half(slot(dy, 1, 0), 0), half(slot(dy, 2, 0), 0), ZM)
+        a = send(part(dy, 1, 0, lo), part(dy, 2, 0, lo), ZM)
+        middle[dy, 0] = len(started)
+        b = send(part(dy, 1, lo, H), part(dy, 2, lo, H), ZM, when=z != 3)
         az[dy]["p", 1].wait_recv()
-        b = send(half(slot(dy, 3, 0), 1), half(slot(dy, 2, 0), 1), ZP)
-        return a, b
+        c = send(part(dy, 3, hi, B), part(dy, 2, hi, B), ZP)
+        middle[dy, 1] = len(started)
+        d = send(part(dy, 3, H, hi), part(dy, 2, H, hi), ZP, when=z != 3)
+        return a, b, c, d
 
     def rest_of_near(dy):
         az[dy]["m", 1].wait_recv()
+        send(part(dy, 1, H, hi), part(dy, 2, H, hi), ZM, when=z == 1, land=middle[dy, 1])
         sib[dy, 1] = to_sibling(dy, 1)
         az[dy]["p", 0].wait_recv()
+        send(part(dy, 3, lo, H), part(dy, 2, lo, H), ZP, when=z == 1, land=middle[dy, 0])
         sib[dy, 3] = to_sibling(dy, 3)
 
     def rest_of_far(dy):
@@ -395,8 +412,10 @@
         for dx in (1, 3, 2):
             npx[p, dx].wait_recv()
     late = [rz, rys[0], *near[0], *(npf[1, dx] for dx in (1, 3, 2))]
-    for copy in started:
-        if not any(copy is other for other in late):
+    for copy, when in started:
+        if when is not None:
+            pl.when(when)(copy.wait_send)
+        elif not any(copy is other for other in late):
             copy.wait_send()
     for p in range(PARTS):
         for dx in (1, 3, 2):

time: 72 us -> 70.7 us (0.982)
  Pallas kernels: 71.2 us -> 69.9 us
    pallas_call x1, Pallas kernels: 66.3 us -> 65 us  [shards(): pl.pallas_call(kernel, out_shape=(pltpu.VMEM((T, K), BF16), pltpu.VMEM((T...]
where the time goes in v4:
time: 70.7 us; the launch traced here: 70.6 us
  Pallas kernels  69.9 us (99%)
    pallas_call x1, Pallas kernels, shards(): pl.pallas_call(kernel, out_shape=(pltpu.VMEM((T, K), BF16), pltpu.VMEM((T...  65 us
    pallas_call x1, Pallas kernels, shards(): pl.pallas_call(finish, out_shape=(out((T, K), BF16), out((T, D), BF16), o...  4.91 us

profile of v4, /device:TPU:0, one launch (start us, length us, event | category | flops | bytes accessed | tf_op | source)
XLA Modules:
  0.0 70.6 jit_solution(3277725122788174211)
XLA Ops:
  0.6 65.0 %window.1 = (bf16[512,512]{1,0:T(8,128)(2,1)S(1)}, bf16[512,8192]{1,0:T(8,128)(2,1)S(1)}, f32[512,512]{1,0:T(8,128)S(1)}, bf16[352,512]{1,0:T(8,128)(2,1)S(1)}, ...) custom-call(bf16[512,8192]{1,0:T(8,128)(2,1)} %tok_hbm.1, ...), custom_call_target="tpu_custom_call" | custom-call | tf_op jit(solution)/shard_map/window/pallas_call | solution.py:460
  65.6 4.9 %finish.1 = (bf16[512,512]{1,0:T(8,128)(2,1)}, bf16[512,8192]{1,0:T(8,128)(2,1)}, f32[1,512,512]{2,1,0:T(8,128)}, f32[1,512]{1,0:T(1,128)}, f32[128,1024]{1,0:T(...) custom-call(bf16[512,512]{1,0:T(8,128)(2,1)S(1)} %get-tuple-element.19.val_v, ...), custom_call_target="tpu_custom_call" | custom-call | tf_op jit(solution)/shard_map/finish/pallas_call | solution.py:512

commit v5 on v4

--- a/solution.py
+++ b/solution.py
@@ -388,8 +388,9 @@
     inner = jnp.sum(cot_v[...].astype(F32) * acc_v, axis=1, keepdims=True)
     inv_v[...] = inv * inv * inv * inner * (1.0 / D)
 
-    lax.fori_loop(0, 8, backward, 0)
+    lax.fori_loop(0, 3, backward, 0)
     spread_params(1)
+    lax.fori_loop(3, 8, backward, 0)
 
     for copy in near[2]:
         copy.wait_recv()

time: 70.7 us -> 70.7 us (level)
  no operation moved by 1% of the time
where the time goes in v5:
time: 70.7 us; the launch traced here: 70.6 us
  Pallas kernels  69.9 us (99%)
    pallas_call x1, Pallas kernels, shards(): pl.pallas_call(kernel, out_shape=(pltpu.VMEM((T, K), BF16), pltpu.VMEM((T...  65 us
    pallas_call x1, Pallas kernels, shards(): pl.pallas_call(finish, out_shape=(out((T, K), BF16), out((T, D), BF16), o...  4.91 us

profile of v5, /device:TPU:0, one launch (start us, length us, event | category | flops | bytes accessed | tf_op | source)
XLA Modules:
  0.0 70.6 jit_solution(6195042920388250431)
XLA Ops:
  0.6 65.0 %window.1 = (bf16[512,512]{1,0:T(8,128)(2,1)S(1)}, bf16[512,8192]{1,0:T(8,128)(2,1)S(1)}, f32[512,512]{1,0:T(8,128)S(1)}, bf16[352,512]{1,0:T(8,128)(2,1)S(1)}, ...) custom-call(bf16[512,8192]{1,0:T(8,128)(2,1)} %tok_hbm.1, ...), custom_call_target="tpu_custom_call" | custom-call | tf_op jit(solution)/shard_map/window/pallas_call | solution.py:461
  65.6 4.9 %finish.1 = (bf16[512,512]{1,0:T(8,128)(2,1)}, bf16[512,8192]{1,0:T(8,128)(2,1)}, f32[1,512,512]{2,1,0:T(8,128)}, f32[1,512]{1,0:T(1,128)}, f32[128,1024]{1,0:T(...) custom-call(bf16[512,512]{1,0:T(8,128)(2,1)S(1)} %get-tuple-element.19.val_v, ...), custom_call_target="tpu_custom_call" | custom-call | tf_op jit(solution)/shard_map/finish/pallas_call | solution.py:513
